TPU v7x, 32 devices: a whole 2x2x4 slice. The times are simulated.
32 devices in a mesh: ctx: 8 (over z, core), tp: 4 (over y, x).
Axes of the slice: x: 2, y: 2, z: 4, core: 2. Of those that a mesh axis runs over, the one named last changes fastest.
Arguments:
- queries: bfloat16 [4096, 2048], P('ctx', 'tp'), may hold values from -6 to 6
- key_rows: bfloat16 [4096, 2048], P('ctx', 'tp'), may hold values from -6 to 6
- value_rows: bfloat16 [4096, 2048], P('ctx', 'tp'), may hold values from -30 to 30
- selection: int32 [8, 3], replicated, may hold values from 0 to 7, as said below
- out_weight: bfloat16 [2048, 7168], P('tp'), may hold values from -0.1875 to 0.1875
Outputs:
- mixed: bfloat16 [4096, 7168], P('ctx', 'tp')
Inputs may be any that keep to these rules, and one draw needn't show every extreme that they name: Row q of selection lists q first, then 3 - 1 distinct blocks below q; where fewer than that lie below q, the remaining entries are q.
All inputs are finite; a program needn't handle non-finite values.
Results may differ from a plain program's by a relative error of at most 0.013.
Values may be sent and summed in bfloat16 or wider, within the bound.
A program may use at most 192 MiB of HBM per device.

v0:
```python
import jax
import jax.numpy as jnp
from jax import lax
from jax.sharding import PartitionSpec as P

HD = 128
BLOCK = 512


neg_fill = -1e30


def per_device(queries, key_rows, value_rows, selection, out_weight):
    row_count, feat_width = queries.shape
    head_count = feat_width // HD
    blocks_here = row_count // BLOCK
    block_total = selection.shape[0]
    ctx_place = lax.axis_index("ctx")
    first_row = ctx_place * row_count
    scaling = 1.0 / jnp.sqrt(jnp.float32(HD))
    query_heads = queries.reshape(row_count, head_count, HD).transpose(1, 0, 2)
    own_choice = lax.dynamic_slice_in_dim(selection, ctx_place * blocks_here, blocks_here, 0)
    repeated = jnp.concatenate(
        [jnp.zeros((blocks_here, 1), bool), own_choice[:, 1:] == own_choice[:, :1]], axis=1
    )
    block_ids = jnp.arange(block_total, dtype=jnp.int32)
    chosen = jnp.any(
        (own_choice[:, :, None] == block_ids[None, None, :])
        & jnp.logical_not(repeated)[:, :, None],
        axis=1,
    )
    query_pos = first_row + jnp.arange(row_count, dtype=jnp.int32)
    initial = (
        jnp.full((head_count, row_count), neg_fill, jnp.float32),
        jnp.zeros((head_count, row_count), jnp.float32),
        jnp.zeros((head_count, row_count, HD), jnp.float32),
    )
    key_piece = lax.all_gather(key_rows, "ctx", axis=0, tiled=True)
    value_piece = lax.all_gather(value_rows, "ctx", axis=0, tiled=True)
    piece_rows = key_piece.shape[0]
    key_pos = jnp.arange(piece_rows, dtype=jnp.int32)
    in_block = (key_pos // BLOCK)[None, :] == block_ids[:, None]
    blockwise = jnp.any(chosen[:, :, None] & in_block[None, :, :], axis=1)
    allowed = jnp.broadcast_to(blockwise[:, None, :], (blocks_here, BLOCK, piece_rows)).reshape(
        row_count, piece_rows
    )
    allowed = allowed & (key_pos[None, :] <= query_pos[:, None])

    def compute(state):
        run_max, run_sum, run_acc = state
        key_heads = key_piece.reshape(piece_rows, head_count, HD).transpose(1, 0, 2)
        value_heads = value_piece.reshape(piece_rows, head_count, HD).transpose(1, 0, 2)
        scores = (
            jnp.einsum("htd,hsd->hts", query_heads, key_heads, preferred_element_type=jnp.float32)
            * scaling
        )
        new_max = jnp.maximum(run_max, jnp.max(jnp.where(allowed[None], scores, neg_fill), axis=-1))
        expo = jnp.where(allowed[None], jnp.exp(scores - new_max[..., None]), 0.0)
        new_sum = jnp.sum(expo, axis=-1)
        weights = expo.astype(jnp.bfloat16)
        new_acc = jnp.einsum(
            "hts,hsd->htd", weights, value_heads, preferred_element_type=jnp.float32
        )
        return (new_max, new_sum, new_acc)

    run_max, run_sum, run_acc = lax.cond(jnp.any(allowed), compute, lambda state: state, initial)
    attended = (
        (run_acc / run_sum[..., None])
        .astype(jnp.bfloat16)
        .transpose(1, 0, 2)
        .reshape(row_count, feat_width)
    )
    columns = lax.all_to_all(out_weight, "tp", split_axis=1, concat_axis=0, tiled=True)
    mixed_out = jnp.dot(
        lax.all_gather(attended, "tp", axis=1, tiled=True),
        columns,
        preferred_element_type=jnp.float32,
    )
    return mixed_out.astype(jnp.bfloat16)


def solution(mesh):
    placed = (P("ctx", "tp"), P("ctx", "tp"), P("ctx", "tp"), P(), P("tp", None))
    return jax.shard_map(
        per_device, mesh=mesh, in_specs=placed, out_specs=P("ctx", "tp"), check_vma=False
    )
```

profile of v0, /device:TPU:25, one launch (start us, length us, event | category | flops | bytes accessed | tf_op | source)
XLA Modules:
  0.0 202.7 jit_solution(10468073287397508878)
XLA Ops:
  6.5 0.0 all-gather.4.cloned.1.call-start
  6.5 0.7 all-gather.4.cloned.1.call-update
  7.3 0.0 all-gather.6.cloned.1.call-start
  7.3 0.7 all-gather.6.cloned.1.call-update
  8.0 10.5 %copy.25 = bf16[512,7168]{0,1:T(8,128)(2,1)} copy(bf16[512,7168]{1,0:T(8,128)(2,1)} %param.11) | data formatting | bytes 14680064 | tf_op args[4]
  18.5 0.0 copy-start.1
  18.5 0.0 copy-start
  18.5 5.5 %all-to-all-start = ((bf16[512,4,1792]{0,2,1:T(8,128)(2,1)}), bf16[512,4,1792]{0,2,1:T(8,128)(2,1)}, u32[]{:S(2)}, u32[]{:S(2)}) async-start(bf16[512,4,1792]{0,2,1:T(8,128)(2,1)} %bitcast.37), calls=%async_computation | async-start | bytes 14680064 | tf_op jit(solution)/shard_map/all_to_all | solution.py:73
  24.0 0.0 all-gather.8.cloned.1.call-start
  24.1 0.0 copy-done.1
  24.1 0.2 fusion.19
  24.3 0.6 slice.7
  24.9 0.0 copy-done
  24.9 1.0 copy.22
  25.9 0.8 compare_reduce_fusion
  26.7 0.1 add_not_fusion
  26.8 0.1 fusion.17
  26.9 0.1 fusion.12
  27.0 3.7 %fusion.10 = (pred[512,4096]{1,0:T(8,128)(4,1)S(1)}, pred[]{:T(512)}) fusion(s32[512]{0:T(512)S(1)} %iota_add_fusion, pred[4096]{0:T(1024)(128)(4,1)S(1)} %fusion.12), kind=kLoop, calls=%fused_computation.15 | loop fusion | flops 6291455 | bytes 2103297 | tf_op jit(solution)/shard_map/and | solution.py:47
  31.4 23.9 %all-gather.4.cloned.1.call-done = bf16[4096,512]{1,0:T(8,128)(2,1)} async-done(((bf16[512,512]{1,0:T(8,128)(2,1)}), bf16[4096,512]{1,0:T(8,128)(2,1)}) %all-gather.4.cloned.1.call-update) | async-done | bytes 4194320 | tf_op jit(solution)/shard_map/all_gather | solution.py:38
  55.3 47.5 %all-gather.6.cloned.1.call-done = bf16[4096,512]{1,0:T(8,128)(2,1)} async-done(((bf16[512,512]{1,0:T(8,128)(2,1)}), bf16[4096,512]{1,0:T(8,128)(2,1)}) %all-gather.6.cloned.1.call-update) | async-done | bytes 4194320 | tf_op jit(solution)/shard_map/all_gather | solution.py:39
  102.8 47.4 %conditional.1 = (f32[4,512]{1,0:T(4,128)S(1)}, f32[4,512,128]{1,2,0:T(8,128)S(1)}) conditional(s32[]{:T(128)} %convert_element_type.12, () %tuple.13, (pred[512,4096]{1,0:T(8,128)(4,1)S(1)}, bf16[4096,512]{1,0:T(8,128)(2,1)}, bf16[4,512,128]{1,2,0:T(8,128)(2,1)}, bf16[4096,512]{1,0:T(8,128)(2,1)}) %tuple.31), branch_computations={%region_3.4_spmd, %region_4.7_spmd} | conditional | flops 4387239936 | bytes 116965392 | solution.py:66
  102.8 16.4 %select_reduce_fusion = (f32[4,512]{1,0:T(4,128)S(1)}, f32[4,512,4096]{2,1,0:T(8,128)}) fusion(pred[512,4096]{1,0:T(8,128)(4,1)S(1)} %get-tuple-element.13, bf16[4,512,128]{1,2,0:T(8,128)(2,1)} %get-tuple-element.31, bf16[4096,512]{1,0:T(8,128)(2,1)} %get-tuple-element.15), kind=kOutput, calls=%fused_computation.1 | convolution fusion | flops 2172647424 | bytes 40378368 | tf_op jit(solution)/shard_map/cond/branch_1_fun/htd,hsd->hts/dot_general | solution.py:54
  119.3 15.6 %fusion.2 = f32[4,512,128]{1,2,0:T(8,128)S(1)} fusion(f32[4,512,4096]{2,1,0:T(8,128)} %get-tuple-element.37, f32[4,512]{1,0:T(4,128)S(1)} %broadcast_maximum_fusion, pred[512,4096]{1,0:T(8,128)(4,1)S(1)} %get-tuple-element.13, bf16[4096,512]{1,0:T(8,128)(2,1)} %get-tuple-element.16), kind=kOutput, calls=%fused_computation.4 | convolution fusion | flops 2181038080 | bytes 40902656 | tf_op jit(solution)/shard_map/cond | solution.py:66
  134.8 15.2 %fusion.1 = f32[4,512]{1,0:T(4,128)S(1)} fusion(f32[4,512,4096]{2,1,0:T(8,128)} %get-tuple-element.37, f32[4,512]{1,0:T(4,128)S(1)} %broadcast_maximum_fusion, pred[512,4096]{1,0:T(8,128)(4,1)S(1)} %get-tuple-element.13), kind=kLoop, calls=%fused_computation.3 | loop fusion | flops 33552384 | bytes 35667968 | tf_op jit(solution)/shard_map/cond/branch_1_fun/reduce_sum | solution.py:59
  150.3 0.9 divide_convert_fusion
  151.2 0.0 all-gather.8.cloned.1.call-update
  151.2 0.0 all-to-all-done
  151.2 10.1 %copy.26 = bf16[4,512,1792]{2,1,0:T(8,128)(2,1)} copy(bf16[4,512,1792]{1,2,0:T(8,128)(2,1)} %bitcast.8) | data formatting | bytes 14680064 | tf_op jit(solution)/shard_map/all_to_all | solution.py:73
  161.4 25.8 %all-gather.8.cloned.1.call-done = bf16[512,2048]{0,1:T(8,128)(2,1)} async-done(((bf16[512,512]{0,1:T(8,128)(2,1)}), bf16[512,2048]{0,1:T(8,128)(2,1)}) %all-gather.8.cloned.1.call-update) | async-done | bytes 2097168 | tf_op jit(solution)/shard_map/all_gather | solution.py:75
  187.2 9.0 %convolution_convert_fusion = bf16[512,1792]{1,0:T(8,128)(2,1)} fusion(bf16[512,2048]{0,1:T(8,128)(2,1)} %all-gather.8.cloned.1.call-done, bf16[2048,1792]{1,0:T(8,128)(2,1)} %bitcast.38), kind=kOutput, calls=%fused_computation.16 | convolution fusion | flops 3759013888 | bytes 11272192 | tf_op jit(solution)/shard_map/dot_general | solution.py:74
  (3 shorter events, 0.0 us)
Async XLA Ops:
  6.5 48.8 %all-gather.4.cloned.1.call-start = ((), (), s32[]{:S(2)}) async-start(), calls=%async_computation.1 | async-start | bytes 4718592 | tf_op jit(solution)/shard_map/all_gather | solution.py:38
  7.3 95.6 %all-gather.6.cloned.1.call-start = ((), (), s32[]{:S(2)}) async-start(), calls=%async_computation.2 | async-start | bytes 4718592 | tf_op jit(solution)/shard_map/all_gather | solution.py:39
  18.5 5.6 %copy-start.1 = (s32[8,3]{0,1:T(4,128)S(1)}, s32[8,3]{0,1:T(4,128)}, u32[]{:S(2)}) copy-start(s32[8,3]{0,1:T(4,128)} %param.10) | copy-start | bytes 292
  18.5 6.4 %copy-start = (bf16[512,512]{1,0:T(8,128)(2,1)S(1)}, bf16[512,512]{1,0:T(8,128)(2,1)}, u32[]{:S(2)}) copy-start(bf16[512,512]{1,0:T(8,128)(2,1)} %param.7) | copy-start | bytes 1572868
  18.5 132.7 %all-to-all-start = ((bf16[512,4,1792]{0,2,1:T(8,128)(2,1)}), bf16[512,4,1792]{0,2,1:T(8,128)(2,1)}, u32[]{:S(2)}, u32[]{:S(2)}) async-start(bf16[512,4,1792]{0,2,1:T(8,128)(2,1)} %bitcast.37), calls=%async_computation | async-start | bytes 14680064 | tf_op jit(solution)/shard_map/all_to_all | solution.py:73
  24.0 163.2 %all-gather.8.cloned.1.call-start = ((), (), s32[]{:S(2)}) async-start(), calls=%async_computation.3 | async-start | bytes 2621440 | tf_op jit(solution)/shard_map/all_gather | solution.py:75
Sparse Core Ops, SparseCore 0:
  9.0 46.3 all-gather.3
  56.9 45.8 all-gather.5
  151.3 35.8 all-gather.7
where the time goes:
time: 205 us; the launch traced here: 203 us
  waiting for transfers between devices  98.7 us (48%)
  matrix products  41 us (20%)
  local copies, waits for them, and re-layouts  22.4 us (11%)
  other arithmetic  21 us (10%)
  between operations  13.8 us (7%)
  starting transfers between devices  5.62 us (3%)
    all_gather x1, waiting for transfers between devices, per_device(): value_piece = lax.all_gather(value_rows, 'ctx', axis=0, tiled=True)  47.5 us
    all_gather x1, waiting for transfers between devices, per_device(): lax.all_gather(attended, 'tp', axis=1, tiled=True)  25.8 us
    all_gather x1, waiting for transfers between devices, per_device(): key_piece = lax.all_gather(key_rows, 'ctx', axis=0, tiled=True)  23.9 us
    dot_general x1, matrix products, compute(): jnp.einsum('htd,hsd->hts', query_heads, key_heads, preferred_element_type...  16.4 us
    cond x1, matrix products, per_device(): lax.cond(jnp.any(allowed), compute, lambda state: state, initial)  15.6 us
    reduce_sum x1, other arithmetic, compute(): new_sum = jnp.sum(expo, axis=-1)  15.2 us
    unnamed x6, local copies, waits for them, and re-layouts  11.5 us
    all_to_all x1, local copies, waits for them, and re-layouts, per_device(): lax.all_to_all(out_weight, 'tp', split_axis=1, concat_axis=0, tiled=True)  10.1 us
  transfers between devices with their start and end apart: 4, of which 3 were waited for; matrix products, arithmetic and copies ran while one was open for 37% of the time, Pallas kernels for 0%

commit v1 on v0

v1 whole, which is shorter than its diff:
```python
import functools

import jax
import jax.numpy as jnp
from jax import lax
from jax.experimental import pallas as pl
from jax.experimental.pallas import tpu as pltpu
from jax.sharding import PartitionSpec as P

HD = 128
BLOCK = 512
NEG = -1e30
MESH = pl.DeviceIdType.MESH
SCALE2 = 1.4426950408889634 / HD**0.5


def kernel(
    n_ctx, n_tp, heads,
    q_ref, k_ref, v_ref, sel_ref, w_ref, out_ref,
    *scratch,
):
    kv = scratch[:heads]
    (wbuf, att, acc, up_send, up_recv, sib_send, sib_recv, w_send, w_recv,
     ws_send, ws_recv, att_send, att_recv) = scratch[heads:]
    chips = n_ctx // 2
    group = heads // 2
    gk = group * HD
    cols = out_ref.shape[1]
    ctx = lax.axis_index("ctx")
    tp = lax.axis_index("tp")
    z, c = ctx // 2, ctx % 2
    sib = z * 2 + 1 - c
    above, below = ctx + 2, ctx - 2
    not_last = z < chips - 1

    barrier = pltpu.get_barrier_semaphore()

    def greet(**where):
        pl.semaphore_signal(barrier, inc=1, device_id=where, device_id_type=MESH)

    greet(ctx=sib)
    for d in range(1, n_tp):
        greet(tp=(tp + d) % n_tp)

    @pl.when(not_last)
    def _():
        greet(ctx=above)

    @pl.when(z > 0)
    def _():
        greet(ctx=below)

    ends = (z == 0).astype(jnp.int32) + (z == chips - 1).astype(jnp.int32)
    pl.semaphore_wait(barrier, n_tp + 2 - ends)

    def remote(src, dst, send, recv, **where):
        return pltpu.make_async_remote_copy(
            src_ref=src, dst_ref=dst, send_sem=send, recv_sem=recv,
            device_id=where, device_id_type=MESH,
        )

    def up(h, zz):
        slot = kv[h].at[zz * 2 + c]
        return remote(slot, slot, up_send.at[h, zz], up_recv.at[h, zz], ctx=above)

    def from_below(h, zz):
        slot = kv[h].at[zz * 2 + c]
        return remote(slot, slot, up_send.at[h, zz], up_recv.at[h, zz], ctx=below)

    def side(h, zz):
        slot = kv[h].at[zz * 2 + c]
        return remote(slot, slot, sib_send.at[h, zz], sib_recv.at[h, zz], ctx=sib)

    def from_side(h, zz):
        slot = kv[h].at[zz * 2 + 1 - c]
        return remote(slot, slot, sib_send.at[h, zz], sib_recv.at[h, zz], ctx=sib)

    def send_on(h, zz):
        @pl.when(not_last)
        def _():
            up(h, zz).start()

        side(h, zz).start()

    def w_rows(half, p):
        return wbuf.at[half, pl.ds(pl.multiple_of(p * gk, gk), gk)]

    def w_out(p):
        src = w_ref.at[pl.ds(pl.multiple_of(c * gk, gk), gk), pl.ds(pl.multiple_of(p * cols, 128), cols)]
        return remote(src, w_rows(c, tp), w_send.at[p], w_recv.at[tp], tp=p)

    def w_in(p):
        return remote(w_rows(c, p), w_rows(c, p), w_send.at[p], w_recv.at[p], tp=p)

    def w_side(p):
        return remote(w_rows(c, p), w_rows(c, p), ws_send.at[p], ws_recv.at[p], ctx=sib)

    def w_from_side(p):
        return remote(w_rows(1 - c, p), w_rows(1 - c, p), ws_send.at[p], ws_recv.at[p], ctx=sib)

    def w_own(half):
        src = w_ref.at[half * gk:(half + 1) * gk, pl.ds(pl.multiple_of(tp * cols, 128), cols)]
        sem = w_send if half == 0 else ws_send
        return pltpu.make_async_copy(src, w_rows(half, tp), sem.at[tp])

    def att_slot(h, p):
        start = p * gk + (h % group) * HD
        return att.at[h // group, :, pl.ds(pl.multiple_of(start, HD), HD)]

    def att_out(h, p):
        return remote(att_slot(h, tp), att_slot(h, tp), att_send.at[h, p], att_recv.at[h, tp], tp=p)

    def att_in(h, p):
        return remote(att_slot(h, p), att_slot(h, p), att_send.at[h, p], att_recv.at[h, p], tp=p)

    peers = [(tp + d) % n_tp for d in range(1, n_tp)]

    def own_block(h):
        kv[h][ctx, 0] = k_ref[:, h * HD:(h + 1) * HD]
        kv[h][ctx, 1] = v_ref[:, h * HD:(h + 1) * HD]
        send_on(h, z)

    own_block(0)
    for p in peers:
        w_out(p).start()
    w_own(0).start()
    w_own(1).start()

    first, second = sel_ref[ctx, 1], sel_ref[ctx, 2]
    bias1 = jnp.where(first == ctx, jnp.float32(NEG), jnp.float32(0))
    bias2 = jnp.where(second == ctx, jnp.float32(NEG), jnp.float32(0))
    contract = (((1,), (1,)), ((), ()))

    def attend(h):
        rows = 256
        k1, v1 = kv[h][first, 0], kv[h][first, 1]
        k2, v2 = kv[h][second, 0], kv[h][second, 1]
        for r in range(BLOCK // rows):
            depth = (r + 1) * rows
            q = q_ref[r * rows:(r + 1) * rows, h * HD:(h + 1) * HD]
            k0 = k_ref[:depth, h * HD:(h + 1) * HD]
            v0 = v_ref[:depth, h * HD:(h + 1) * HD]

            def score(k):
                return lax.dot_general(q, k, contract, preferred_element_type=jnp.float32)

            s0, s1, s2 = score(k0), score(k1) + bias1, score(k2) + bias2
            rid = lax.broadcasted_iota(jnp.int32, s0.shape, 0) + r * rows
            cid = lax.broadcasted_iota(jnp.int32, s0.shape, 1)
            s0 = jnp.where(cid <= rid, s0, NEG)
            top = jnp.maximum(
                jnp.max(s0, axis=1, keepdims=True),
                jnp.maximum(jnp.max(s1, axis=1, keepdims=True), jnp.max(s2, axis=1, keepdims=True)),
            )
            e0, e1, e2 = (jnp.exp2((s - top) * SCALE2) for s in (s0, s1, s2))
            total = (
                jnp.sum(e0, axis=1, keepdims=True)
                + jnp.sum(e1, axis=1, keepdims=True)
                + jnp.sum(e2, axis=1, keepdims=True)
            )
            numer = sum(
                jnp.dot(e.astype(jnp.bfloat16), v, preferred_element_type=jnp.float32)
                for e, v in ((e0, v0), (e1, v1), (e2, v2))
            )
            start = pl.multiple_of(tp * gk + (h % group) * HD, HD)
            att[h // group, r * rows:(r + 1) * rows, pl.ds(start, HD)] = (numer / total).astype(jnp.bfloat16)
        for p in peers:
            att_out(h, p).start()

    tile = 256 if cols % 256 == 0 else 128

    def project(g):
        for h in range(g * group, (g + 1) * group):
            for p in peers:
                att_in(h, p).wait_recv()

        @pl.loop(0, cols // tile)
        def _(n):
            at = pl.ds(pl.multiple_of(n * tile, tile), tile)
            part = jnp.dot(att[g], wbuf[g, :, at], preferred_element_type=jnp.float32)
            if g == 0:
                acc[:, at] = part
            else:
                out_ref[:, at] = (acc[:, at] + part).astype(out_ref.dtype)

    for h in range(heads):
        if h + 1 < heads:
            own_block(h + 1)
        if h == heads - 1:
            for p in peers:
                w_in(p).wait_recv()
                w_side(p).start()

        @pl.loop(0, z)
        def _(s):
            zz = z - 1 - s
            from_below(h, zz).wait_recv()
            send_on(h, zz)

        if h == heads - 1:
            w_own(0).wait()
            w_own(1).wait()
            for p in peers:
                w_from_side(p).wait_recv()
            project(0)

        @pl.loop(0, z + 1)
        def _(zz):
            from_side(h, zz).wait_recv()

        attend(h)
    project(1)

    for h in range(heads):
        @pl.loop(0, z + 1)
        def _(zz):
            side(h, zz).wait_send()

            @pl.when(not_last)
            def _():
                up(h, zz).wait_send()

        for p in peers:
            att_out(h, p).wait_send()
    for p in peers:
        w_out(p).wait_send()
        w_side(p).wait_send()


def per_device(n_ctx, n_tp, queries, key_rows, value_rows, selection, out_weight):
    rows, width = queries.shape
    heads = width // HD
    cols = out_weight.shape[1] // n_tp
    gk = heads // 2 * HD
    chips = n_ctx // 2
    vmem = pl.BlockSpec(memory_space=pltpu.VMEM)
    dma = pltpu.SemaphoreType.DMA
    return pl.pallas_call(
        functools.partial(kernel, n_ctx, n_tp, heads),
        out_shape=jax.ShapeDtypeStruct((rows, cols), jnp.bfloat16),
        in_specs=[
            vmem, vmem, vmem,
            pl.BlockSpec(memory_space=pltpu.SMEM),
            pl.BlockSpec(memory_space=pl.ANY),
        ],
        out_specs=vmem,
        scratch_shapes=[pltpu.VMEM((n_ctx, 2, BLOCK, HD), jnp.bfloat16) for _ in range(heads)] + [
            pltpu.VMEM((2, n_tp * gk, cols), jnp.bfloat16),
            pltpu.VMEM((2, rows, n_tp * gk), jnp.bfloat16),
            pltpu.VMEM((rows, cols), jnp.float32),
            dma((heads, chips)), dma((heads, chips)),
            dma((heads, chips)), dma((heads, chips)),
            dma((n_tp,)), dma((n_tp,)), dma((n_tp,)), dma((n_tp,)),
            dma((heads, n_tp)), dma((heads, n_tp)),
        ],
        compiler_params=pltpu.CompilerParams(
            collective_id=0, has_side_effects=True, vmem_limit_bytes=52 * 2**20
        ),
        cost_estimate=pl.CostEstimate(
            flops=2 * rows * cols * n_tp * width + 12 * rows * BLOCK * width,
            bytes_accessed=2 * (out_weight.size + 4 * rows * width),
            transcendentals=3 * rows * BLOCK * heads,
        ),
    )(queries, key_rows, value_rows, selection, out_weight)


def solution(mesh):
    placed = (P("ctx", "tp"), P("ctx", "tp"), P("ctx", "tp"), P(), P("tp", None))
    body = functools.partial(per_device, mesh.shape["ctx"], mesh.shape["tp"])
    return jax.shard_map(
        body, mesh=mesh, in_specs=placed, out_specs=P("ctx", "tp"), check_vma=False
    )
```

time: 205 us -> 95.8 us (0.47)
  waiting for transfers between devices: 98.7 us -> 0 us
  Pallas kernels: 0 us -> 88 us
  matrix products: 41 us -> 0 us
  other arithmetic: 21 us -> 0 us
  local copies, waits for them, and re-layouts: 22.4 us -> 6.72 us
  between operations: 13.8 us -> 0.01 us
  starting transfers between devices: 5.62 us -> 0 us
    all_gather x3 -> x0, waiting for transfers between devices: 97.2 us -> none  [the longest x1 47.5 us: per_device(): value_piece = lax.all_gather(value_rows, 'ctx', axis=0, tiled=True)]
    pallas_call x0 -> x1, Pallas kernels: none -> 88 us  [per_device(): pl.pallas_call(functools.partial(kernel, n_ctx, n_tp, heads), out_shape=j...]
    dot_general x2 -> x0, matrix products: 25.4 us -> none  [the longest x1 16.4 us: compute(): jnp.einsum('htd,hsd->hts', query_heads, key_heads, preferred_element_type...]
    cond x1 -> x0, matrix products: 15.6 us -> none  [per_device(): lax.cond(jnp.any(allowed), compute, lambda state: state, initial)]
    reduce_sum x1 -> x0, other arithmetic: 15.2 us -> none  [compute(): new_sum = jnp.sum(expo, axis=-1)]
    all_to_all x1 -> x0, local copies, waits for them, and re-layouts: 10.1 us -> none  [per_device(): lax.all_to_all(out_weight, 'tp', split_axis=1, concat_axis=0, tiled=True)]
    all_to_all x1 -> x0, starting transfers between devices: 5.54 us -> none  [per_device(): lax.all_to_all(out_weight, 'tp', split_axis=1, concat_axis=0, tiled=True)]
    unnamed x6 -> x8, local copies, waits for them, and re-layouts: 11.5 us -> 6.72 us
  transfers between devices with their start and end apart: 4 -> 0, of which waited for: 3 -> 0; matrix products, arithmetic and copies ran while one was open for 37% -> 0% of each run, Pallas kernels for 0% -> 0%
where the time goes in v1:
time: 95.8 us; the launch traced here: 94.8 us
  Pallas kernels  88 us (92%)
  local copies, waits for them, and re-layouts  6.72 us (7%)
    pallas_call x1, Pallas kernels, per_device(): pl.pallas_call(functools.partial(kernel, n_ctx, n_tp, heads), out_shape=j...  88 us
    unnamed x8, local copies, waits for them, and re-layouts  6.72 us

profile of v1, /device:TPU:25, one launch (start us, length us, event | category | flops | bytes accessed | tf_op | source)
XLA Modules:
  0.0 94.8 jit_solution(52003736877212191)
XLA Ops:
  0.0 0.8 copy.6.sel_ref
  0.8 0.0 copy-start
  0.8 1.0 %copy-done = bf16[512,512]{1,0:T(8,128)(2,1)S(1)} copy-done((bf16[512,512]{1,0:T(8,128)(2,1)S(1)}, bf16[512,512]{1,0:T(8,128)(2,1)}, u32[]{:S(2)}) %copy-start) | copy-done | bytes 524312
  1.8 0.0 copy-start.1
  1.8 1.0 %copy-done.1 = bf16[512,512]{1,0:T(8,128)(2,1)S(1)} copy-done((bf16[512,512]{1,0:T(8,128)(2,1)S(1)}, bf16[512,512]{1,0:T(8,128)(2,1)}, u32[]{:S(2)}) %copy-start.1) | copy-done | bytes 524312
  2.8 0.0 copy-start.2
  2.8 1.0 %copy-done.2 = bf16[512,512]{1,0:T(8,128)(2,1)S(1)} copy-done((bf16[512,512]{1,0:T(8,128)(2,1)S(1)}, bf16[512,512]{1,0:T(8,128)(2,1)}, u32[]{:S(2)}) %copy-start.2) | copy-done | bytes 524312
  3.9 88.0 %shard_map.55 = bf16[512,1792]{1,0:T(8,128)(2,1)} custom-call(bf16[512,512]{1,0:T(8,128)(2,1)S(1)} %copy-done, bf16[512,512]{1,0:T(8,128)(2,1)S(1)} %copy-done.1, bf16[512,512]{1,0:T(8,128)(2,1)S(1)} %copy-done.2, s32[8,3]{1,0:T(8,128)S(1)} %copy.6.sel_ref, bf16[512,7168]{1,0:T(8,128)(2,1)} %w_ref.1), custom_call_target="tpu_custom_call" | custom-call | flops 5368709120 | bytes 9437184 | tf_op jit(solution)/shard_map/pallas_call | solution.py:238
  91.9 2.8 %copy.8 = bf16[512,1792]{1,0:T(8,128)(2,1)} copy(bf16[512,1792]{1,0:T(8,128)(2,1)} %shard_map.55) | data formatting | bytes 3670016
Async XLA Ops:
  0.8 1.0 %copy-start = (bf16[512,512]{1,0:T(8,128)(2,1)S(1)}, bf16[512,512]{1,0:T(8,128)(2,1)}, u32[]{:S(2)}) copy-start(bf16[512,512]{1,0:T(8,128)(2,1)} %q_ref.1) | copy-start | bytes 1572868
  1.8 1.0 %copy-start.1 = (bf16[512,512]{1,0:T(8,128)(2,1)S(1)}, bf16[512,512]{1,0:T(8,128)(2,1)}, u32[]{:S(2)}) copy-start(bf16[512,512]{1,0:T(8,128)(2,1)} %k_ref.1) | copy-start | bytes 1572868
  2.8 1.0 %copy-start.2 = (bf16[512,512]{1,0:T(8,128)(2,1)S(1)}, bf16[512,512]{1,0:T(8,128)(2,1)}, u32[]{:S(2)}) copy-start(bf16[512,512]{1,0:T(8,128)(2,1)} %v_ref.1) | copy-start | bytes 1572868

commit v2 on v1

--- a/solution.py
+++ b/solution.py
@@ -10,18 +10,20 @@
 HD = 128
 BLOCK = 512
 NEG = -1e30
+PARTS = 8
 MESH = pl.DeviceIdType.MESH
 SCALE2 = 1.4426950408889634 / HD**0.5
 
 
 def kernel(
     n_ctx, n_tp, heads,
-    q_ref, k_ref, v_ref, sel_ref, w_ref, out_ref,
+    q_hbm, k_hbm, v_hbm, sel_ref, w_ref, out_ref,
     *scratch,
 ):
     kv = scratch[:heads]
-    (wbuf, att, acc, up_send, up_recv, sib_send, sib_recv, w_send, w_recv,
-     ws_send, ws_recv, att_send, att_recv) = scratch[heads:]
+    stage = scratch[heads:2 * heads]
+    (q_ref, wbuf, att, acc, up_send, up_recv, sib_send, sib_recv, w_send, w_recv,
+     ws_send, ws_recv, att_send, att_recv, in_sem) = scratch[2 * heads:]
     chips = n_ctx // 2
     group = heads // 2
     gk = group * HD
@@ -32,6 +34,20 @@
     sib = z * 2 + 1 - c
     above, below = ctx + 2, ctx - 2
     not_last = z < chips - 1
+    chained = z < chips - 2
+    packs = z == chips - 2
+
+    def load_q():
+        return pltpu.make_async_copy(q_hbm, q_ref, in_sem.at[2, 0])
+
+    def load_kv(h, part):
+        src = (k_hbm, v_hbm)[part].at[:, h * HD:(h + 1) * HD]
+        return pltpu.make_async_copy(src, kv[h].at[ctx, part], in_sem.at[part, h])
+
+    for h in range(heads):
+        load_kv(h, 0).start()
+        load_kv(h, 1).start()
+    load_q().start()
 
     barrier = pltpu.get_barrier_semaphore()
 
@@ -76,11 +92,20 @@
         return remote(slot, slot, sib_send.at[h, zz], sib_recv.at[h, zz], ctx=sib)
 
     def send_on(h, zz):
-        @pl.when(not_last)
+        @pl.when(chained)
         def _():
             up(h, zz).start()
 
         side(h, zz).start()
+
+    def packed(h, where):
+        return remote(stage[h], kv[h].at[pl.ds(0, 2)], up_send.at[h, 0], up_recv.at[h, 0], ctx=where)
+
+    def pack(h):
+        for slot in range(2):
+            want = sel_ref[slot + 1, above]
+            stage[h][slot] = kv[h][jnp.where(want < 2 * (z + 1), want, ctx)]
+        packed(h, above).start()
 
     def w_rows(half, p):
         return wbuf.at[half, pl.ds(pl.multiple_of(p * gk, gk), gk)]
@@ -116,8 +141,8 @@
     peers = [(tp + d) % n_tp for d in range(1, n_tp)]
 
     def own_block(h):
-        kv[h][ctx, 0] = k_ref[:, h * HD:(h + 1) * HD]
-        kv[h][ctx, 1] = v_ref[:, h * HD:(h + 1) * HD]
+        load_kv(h, 0).wait()
+        load_kv(h, 1).wait()
         send_on(h, z)
 
     own_block(0)
@@ -126,9 +151,12 @@
     w_own(0).start()
     w_own(1).start()
 
-    first, second = sel_ref[ctx, 1], sel_ref[ctx, 2]
+    first, second = sel_ref[1, ctx], sel_ref[2, ctx]
     bias1 = jnp.where(first == ctx, jnp.float32(NEG), jnp.float32(0))
     bias2 = jnp.where(second == ctx, jnp.float32(NEG), jnp.float32(0))
+    near = jnp.where(not_last, 0, 2 * z)
+    first = jnp.where(first >= near, first, 0)
+    second = jnp.where(second >= near, second, 1)
     contract = (((1,), (1,)), ((), ()))
 
     def attend(h):
@@ -138,8 +166,8 @@
         for r in range(BLOCK // rows):
             depth = (r + 1) * rows
             q = q_ref[r * rows:(r + 1) * rows, h * HD:(h + 1) * HD]
-            k0 = k_ref[:depth, h * HD:(h + 1) * HD]
-            v0 = v_ref[:depth, h * HD:(h + 1) * HD]
+            k0 = kv[h][ctx, 0, :depth]
+            v0 = kv[h][ctx, 1, :depth]
 
             def score(k):
                 return lax.dot_general(q, k, contract, preferred_element_type=jnp.float32)
@@ -183,48 +211,85 @@
             else:
                 out_ref[:, at] = (acc[:, at] + part).astype(out_ref.dtype)
 
+    def first_half():
+        for p in peers:
+            w_in(p).wait_recv()
+            w_side(p).start()
+        w_own(0).wait()
+        w_own(1).wait()
+        for p in peers:
+            w_from_side(p).wait_recv()
+        project(0)
+
+    load_q().wait()
     for h in range(heads):
         if h + 1 < heads:
             own_block(h + 1)
         if h == heads - 1:
-            for p in peers:
-                w_in(p).wait_recv()
-                w_side(p).start()
-
-        @pl.loop(0, z)
-        def _(s):
-            zz = z - 1 - s
-            from_below(h, zz).wait_recv()
-            send_on(h, zz)
-
-        if h == heads - 1:
-            w_own(0).wait()
-            w_own(1).wait()
-            for p in peers:
-                w_from_side(p).wait_recv()
-            project(0)
-
-        @pl.loop(0, z + 1)
-        def _(zz):
-            from_side(h, zz).wait_recv()
+            pl.when(z == chips - 1)(first_half)
+
+        @pl.when(not_last)
+        def _():
+            @pl.loop(0, z)
+            def _(s):
+                zz = z - 1 - s
+                from_below(h, zz).wait_recv()
+                send_on(h, zz)
+
+            @pl.loop(0, z)
+            def _(zz):
+                from_side(h, zz).wait_recv()
+
+        from_side(h, z).wait_recv()
+
+        @pl.when(packs)
+        def _():
+            pack(h)
+
+        @pl.when(z == chips - 1)
+        def _():
+            packed(h, below).wait_recv()
 
         attend(h)
+    pl.when(not_last)(first_half)
     project(1)
 
     for h in range(heads):
-        @pl.loop(0, z + 1)
-        def _(zz):
-            side(h, zz).wait_send()
-
-            @pl.when(not_last)
-            def _():
+        side(h, z).wait_send()
+
+        @pl.when(not_last)
+        def _():
+            @pl.loop(0, z)
+            def _(zz):
+                side(h, zz).wait_send()
+
+        @pl.when(chained)
+        def _():
+            @pl.loop(0, z + 1)
+            def _(zz):
                 up(h, zz).wait_send()
+
+        @pl.when(packs)
+        def _():
+            packed(h, above).wait_send()
 
         for p in peers:
             att_out(h, p).wait_send()
     for p in peers:
         w_out(p).wait_send()
         w_side(p).wait_send()
+
+
+def hand_over(src, dst, sem):
+    step = src.shape[0] // PARTS
+    copies = [
+        pltpu.make_async_copy(src.at[n * step:(n + 1) * step], dst.at[n * step:(n + 1) * step], sem.at[n])
+        for n in range(PARTS)
+    ]
+    for copy in copies:
+        copy.start()
+    for copy in copies:
+        copy.wait()
 
 
 def per_device(n_ctx, n_tp, queries, key_rows, value_rows, selection, out_weight):
@@ -234,17 +299,20 @@
     gk = heads // 2 * HD
     chips = n_ctx // 2
     vmem = pl.BlockSpec(memory_space=pltpu.VMEM)
+    hbm = pl.BlockSpec(memory_space=pl.ANY)
     dma = pltpu.SemaphoreType.DMA
-    return pl.pallas_call(
+    held = pl.pallas_call(
         functools.partial(kernel, n_ctx, n_tp, heads),
         out_shape=jax.ShapeDtypeStruct((rows, cols), jnp.bfloat16),
         in_specs=[
-            vmem, vmem, vmem,
+            hbm, hbm, hbm,
             pl.BlockSpec(memory_space=pltpu.SMEM),
-            pl.BlockSpec(memory_space=pl.ANY),
+            hbm,
         ],
         out_specs=vmem,
-        scratch_shapes=[pltpu.VMEM((n_ctx, 2, BLOCK, HD), jnp.bfloat16) for _ in range(heads)] + [
+        scratch_shapes=[pltpu.VMEM((n_ctx, 2, BLOCK, HD), jnp.bfloat16) for _ in range(heads)]
+        + [pltpu.VMEM((2, 2, BLOCK, HD), jnp.bfloat16) for _ in range(heads)] + [
+            pltpu.VMEM((rows, width), jnp.bfloat16),
             pltpu.VMEM((2, n_tp * gk, cols), jnp.bfloat16),
             pltpu.VMEM((2, rows, n_tp * gk), jnp.bfloat16),
             pltpu.VMEM((rows, cols), jnp.float32),
@@ -252,6 +320,7 @@
             dma((heads, chips)), dma((heads, chips)),
             dma((n_tp,)), dma((n_tp,)), dma((n_tp,)), dma((n_tp,)),
             dma((heads, n_tp)), dma((heads, n_tp)),
+            dma((3, heads)),
         ],
         compiler_params=pltpu.CompilerParams(
             collective_id=0, has_side_effects=True, vmem_limit_bytes=52 * 2**20
@@ -261,7 +330,14 @@
             bytes_accessed=2 * (out_weight.size + 4 * rows * width),
             transcendentals=3 * rows * BLOCK * heads,
         ),
-    )(queries, key_rows, value_rows, selection, out_weight)
+    )(queries, key_rows, value_rows, selection.T, out_weight)
+    return pl.pallas_call(
+        hand_over,
+        out_shape=jax.ShapeDtypeStruct((rows, cols), jnp.bfloat16),
+        in_specs=[hbm],
+        out_specs=hbm,
+        scratch_shapes=[dma((PARTS,))],
+    )(held)
 
 
 def solution(mesh):

time: 95.8 us -> 144 us (1.50)
  Pallas kernels: 88 us -> 140 us
  local copies, waits for them, and re-layouts: 6.72 us -> 3.8 us
    pallas_call x0 -> x1, Pallas kernels: none -> 56.8 us  [per_device(): pl.pallas_call(hand_over, out_shape=jax.ShapeDtypeStruct((rows, cols), jn...]
    pallas_call x1, Pallas kernels: 88 us -> 83.4 us  [per_device(): pl.pallas_call(functools.partial(kernel, n_ctx, n_tp, heads), out_shape=j...]
    unnamed x8, local copies, waits for them, and re-layouts: 6.72 us -> 3.8 us
where the time goes in v2:
time: 144 us
  Pallas kernels  140 us (97%)
  local copies, waits for them, and re-layouts  3.8 us (3%)
    pallas_call x1, Pallas kernels, per_device(): pl.pallas_call(functools.partial(kernel, n_ctx, n_tp, heads), out_shape=j...  83.4 us
    pallas_call x1, Pallas kernels, per_device(): pl.pallas_call(hand_over, out_shape=jax.ShapeDtypeStruct((rows, cols), jn...  56.8 us
    unnamed x8, local copies, waits for them, and re-layouts  3.8 us

profile of v2, /device:TPU:25, one launch (start us, length us, event | category | flops | bytes accessed | tf_op | source)
XLA Modules:
  0.0 143.9 jit_solution(320627348016474942)
XLA Ops:
  0.0 0.0 copy-start
  0.0 1.0 copy-done
  1.0 0.0 copy-start.1
  1.0 1.0 copy-done.1
  2.1 0.0 copy-start.2
  2.1 1.0 copy-done.2
  3.1 0.0 copy-start.3
  3.1 0.7 copy-done.3
  3.8 83.4 %shard_map.55.src = bf16[512,1792]{1,0:T(8,128)(2,1)} custom-call(bf16[512,512]{1,0:T(8,128)(2,1)S(1)} %copy-done, bf16[512,512]{1,0:T(8,128)(2,1)S(1)} %copy-done.1, bf16[512,512]{1,0:T(8,128)(2,1)S(1)} %copy-done.2, s32[3,8]{1,0:T(4,128)S(1)} %bitcast.1, bf16[512,7168]{1,0:T(8,128)(2,1)} %w_ref.1), custom_call_target="tpu_custom_call" | custom-call | flops 5368709120 | bytes 9437184 | tf_op jit(solution)/shard_map/pallas_call | solution.py:304
  87.2 56.8 %shard_map.56 = bf16[512,1792]{1,0:T(8,128)(2,1)} custom-call(bf16[512,1792]{1,0:T(8,128)(2,1)} %shard_map.55.src), custom_call_target="tpu_custom_call" | custom-call | tf_op jit(solution)/shard_map/pallas_call | solution.py:334
Async XLA Ops:
  0.0 1.0 copy-start
  1.0 1.0 copy-start.1
  2.1 1.0 copy-start.2
  3.1 0.7 copy-start.3

commit v3 on v2

--- a/solution.py
+++ b/solution.py
@@ -20,10 +20,11 @@
     q_hbm, k_hbm, v_hbm, sel_ref, w_ref, out_ref,
     *scratch,
 ):
-    kv = scratch[:heads]
-    stage = scratch[heads:2 * heads]
+    units = 2 * heads
+    kv = scratch[:units]
+    stage = scratch[units:2 * units]
     (q_ref, wbuf, att, acc, up_send, up_recv, sib_send, sib_recv, w_send, w_recv,
-     ws_send, ws_recv, att_send, att_recv, in_sem) = scratch[2 * heads:]
+     ws_send, ws_recv, att_send, att_recv, in_sem) = scratch[2 * units:]
     chips = n_ctx // 2
     group = heads // 2
     gk = group * HD
@@ -42,7 +43,7 @@
 
     def load_kv(h, part):
         src = (k_hbm, v_hbm)[part].at[:, h * HD:(h + 1) * HD]
-        return pltpu.make_async_copy(src, kv[h].at[ctx, part], in_sem.at[part, h])
+        return pltpu.make_async_copy(src, kv[2 * h + part].at[ctx], in_sem.at[part, h])
 
     for h in range(heads):
         load_kv(h, 0).start()
@@ -75,37 +76,37 @@
             device_id=where, device_id_type=MESH,
         )
 
-    def up(h, zz):
-        slot = kv[h].at[zz * 2 + c]
-        return remote(slot, slot, up_send.at[h, zz], up_recv.at[h, zz], ctx=above)
-
-    def from_below(h, zz):
-        slot = kv[h].at[zz * 2 + c]
-        return remote(slot, slot, up_send.at[h, zz], up_recv.at[h, zz], ctx=below)
-
-    def side(h, zz):
-        slot = kv[h].at[zz * 2 + c]
-        return remote(slot, slot, sib_send.at[h, zz], sib_recv.at[h, zz], ctx=sib)
-
-    def from_side(h, zz):
-        slot = kv[h].at[zz * 2 + 1 - c]
-        return remote(slot, slot, sib_send.at[h, zz], sib_recv.at[h, zz], ctx=sib)
-
-    def send_on(h, zz):
+    def up(u, zz):
+        slot = kv[u].at[zz * 2 + c]
+        return remote(slot, slot, up_send.at[u, zz], up_recv.at[u, zz], ctx=above)
+
+    def from_below(u, zz):
+        slot = kv[u].at[zz * 2 + c]
+        return remote(slot, slot, up_send.at[u, zz], up_recv.at[u, zz], ctx=below)
+
+    def side(u, zz):
+        slot = kv[u].at[zz * 2 + c]
+        return remote(slot, slot, sib_send.at[u, zz], sib_recv.at[u, zz], ctx=sib)
+
+    def from_side(u, zz):
+        slot = kv[u].at[zz * 2 + 1 - c]
+        return remote(slot, slot, sib_send.at[u, zz], sib_recv.at[u, zz], ctx=sib)
+
+    def send_on(u, zz):
         @pl.when(chained)
         def _():
-            up(h, zz).start()
-
-        side(h, zz).start()
-
-    def packed(h, where):
-        return remote(stage[h], kv[h].at[pl.ds(0, 2)], up_send.at[h, 0], up_recv.at[h, 0], ctx=where)
-
-    def pack(h):
+            up(u, zz).start()
+
+        side(u, zz).start()
+
+    def packed(u, where):
+        return remote(stage[u], kv[u].at[pl.ds(0, 2)], up_send.at[u, 0], up_recv.at[u, 0], ctx=where)
+
+    def pack(u):
         for slot in range(2):
             want = sel_ref[slot + 1, above]
-            stage[h][slot] = kv[h][jnp.where(want < 2 * (z + 1), want, ctx)]
-        packed(h, above).start()
+            stage[u][slot] = kv[u][jnp.where(want < 2 * (z + 1), want, ctx)]
+        packed(u, above).start()
 
     def w_rows(half, p):
         return wbuf.at[half, pl.ds(pl.multiple_of(p * gk, gk), gk)]
@@ -138,14 +139,36 @@
     def att_in(h, p):
         return remote(att_slot(h, p), att_slot(h, p), att_send.at[h, p], att_recv.at[h, p], tp=p)
 
-    peers = [(tp + d) % n_tp for d in range(1, n_tp)]
-
-    def own_block(h):
-        load_kv(h, 0).wait()
-        load_kv(h, 1).wait()
-        send_on(h, z)
+    relay = n_tp == 4
+    if relay:
+        tx, ty = tp % 2, tp // 2
+        px, py, pd = ty * 2 + 1 - tx, (1 - ty) * 2 + tx, (1 - ty) * 2 + 1 - tx
+        peers = [px, py, pd]
+    else:
+        peers = [(tp + d) % n_tp for d in range(1, n_tp)]
+
+    def relayed(h):
+        return relay and h < heads - 1
+
+    def att_relay(h):
+        owner, target = (px, py) if h % 2 == 0 else (py, px)
+        return remote(att_slot(h, owner), att_slot(h, owner), att_send.at[h, pd], att_recv.at[h, owner], tp=target)
+
+    def pass_on(h):
+        if relayed(h):
+            att_in(h, px if h % 2 == 0 else py).wait_recv()
+            att_relay(h).start()
+
+    def await_att(h, n):
+        if not (relayed(h) and n == h % 2):
+            att_in(h, peers[n]).wait_recv()
+
+    def own_block(u):
+        load_kv(u // 2, u % 2).wait()
+        send_on(u, z)
 
     own_block(0)
+    own_block(1)
     for p in peers:
         w_out(p).start()
     w_own(0).start()
@@ -161,13 +184,13 @@
 
     def attend(h):
         rows = 256
-        k1, v1 = kv[h][first, 0], kv[h][first, 1]
-        k2, v2 = kv[h][second, 0], kv[h][second, 1]
+        k1, v1 = kv[2 * h][first], kv[2 * h + 1][first]
+        k2, v2 = kv[2 * h][second], kv[2 * h + 1][second]
         for r in range(BLOCK // rows):
             depth = (r + 1) * rows
             q = q_ref[r * rows:(r + 1) * rows, h * HD:(h + 1) * HD]
-            k0 = kv[h][ctx, 0, :depth]
-            v0 = kv[h][ctx, 1, :depth]
+            k0 = kv[2 * h][ctx, :depth]
+            v0 = kv[2 * h + 1][ctx, :depth]
 
             def score(k):
                 return lax.dot_general(q, k, contract, preferred_element_type=jnp.float32)
@@ -192,15 +215,15 @@
             )
             start = pl.multiple_of(tp * gk + (h % group) * HD, HD)
             att[h // group, r * rows:(r + 1) * rows, pl.ds(start, HD)] = (numer / total).astype(jnp.bfloat16)
-        for p in peers:
+        for p in peers[:2] if relayed(h) else peers:
             att_out(h, p).start()
 
     tile = 256 if cols % 256 == 0 else 128
 
     def project(g):
         for h in range(g * group, (g + 1) * group):
-            for p in peers:
-                att_in(h, p).wait_recv()
+            for n in range(n_tp - 1):
+                await_att(h, n)
 
         @pl.loop(0, cols // tile)
         def _(n):
@@ -221,75 +244,113 @@
             w_from_side(p).wait_recv()
         project(0)
 
+    def add_rows(p, opening=False, closing=False):
+        at_p = pl.ds(pl.multiple_of(p * gk, gk), gk)
+
+        @pl.loop(0, cols // tile)
+        def _(n):
+            at = pl.ds(pl.multiple_of(n * tile, tile), tile)
+            part = sum(
+                jnp.dot(att[g, :, at_p], wbuf[g, at_p, at], preferred_element_type=jnp.float32)
+                for g in range(2)
+            )
+            if not opening:
+                part = part + acc[:, at]
+            if closing:
+                out_ref[:, at] = part.astype(out_ref.dtype)
+            else:
+                acc[:, at] = part
+
+    def by_peer():
+        for h in range(heads):
+            pass_on(h)
+        w_own(0).wait()
+        w_own(1).wait()
+
+        def add_peer(n):
+            w_from_side(peers[n]).wait_recv()
+            for h in range(heads):
+                await_att(h, n)
+            add_rows(peers[n], closing=n == n_tp - 2)
+
+        for n in range(n_tp - 1):
+            w_in(peers[n]).wait_recv()
+            w_side(peers[n]).start()
+            if n == 0:
+                add_rows(tp, opening=True)
+            else:
+                add_peer(n - 1)
+        add_peer(n_tp - 2)
+
+    is_last = z == chips - 1
     load_q().wait()
-    for h in range(heads):
-        if h + 1 < heads:
-            own_block(h + 1)
-        if h == heads - 1:
-            pl.when(z == chips - 1)(first_half)
+    for u in range(units):
+        h = u // 2
+        if u + 2 < units:
+            own_block(u + 2)
+        if u == units - 2:
+            pl.when(is_last)(first_half)
 
         @pl.when(not_last)
         def _():
             @pl.loop(0, z)
             def _(s):
                 zz = z - 1 - s
-                from_below(h, zz).wait_recv()
-                send_on(h, zz)
+                from_below(u, zz).wait_recv()
+                send_on(u, zz)
 
             @pl.loop(0, z)
             def _(zz):
-                from_side(h, zz).wait_recv()
-
-        from_side(h, z).wait_recv()
+                from_side(u, zz).wait_recv()
+
+        from_side(u, z).wait_recv()
 
         @pl.when(packs)
         def _():
-            pack(h)
-
-        @pl.when(z == chips - 1)
-        def _():
-            packed(h, below).wait_recv()
-
-        attend(h)
-    pl.when(not_last)(first_half)
-    project(1)
-
-    for h in range(heads):
-        side(h, z).wait_send()
+            pack(u)
+
+        @pl.when(is_last)
+        def _():
+            packed(u, below).wait_recv()
+
+        if u % 2 == 1:
+            if h >= 1:
+                pl.when(is_last)(functools.partial(pass_on, h - 1))
+            attend(h)
+    pl.when(is_last)(functools.partial(project, 1))
+    pl.when(not_last)(by_peer)
+
+    for u in range(units):
+        side(u, z).wait_send()
 
         @pl.when(not_last)
         def _():
             @pl.loop(0, z)
             def _(zz):
-                side(h, zz).wait_send()
+                side(u, zz).wait_send()
 
         @pl.when(chained)
         def _():
             @pl.loop(0, z + 1)
             def _(zz):
-                up(h, zz).wait_send()
+                up(u, zz).wait_send()
 
         @pl.when(packs)
         def _():
-            packed(h, above).wait_send()
-
-        for p in peers:
+            packed(u, above).wait_send()
+
+    for h in range(heads):
+        for p in peers[:2] if relayed(h) else peers:
             att_out(h, p).wait_send()
+        if relayed(h):
+            att_relay(h).wait_send()
     for p in peers:
         w_out(p).wait_send()
         w_side(p).wait_send()
 
 
-def hand_over(src, dst, sem):
-    step = src.shape[0] // PARTS
-    copies = [
-        pltpu.make_async_copy(src.at[n * step:(n + 1) * step], dst.at[n * step:(n + 1) * step], sem.at[n])
-        for n in range(PARTS)
-    ]
-    for copy in copies:
-        copy.start()
-    for copy in copies:
-        copy.wait()
+def hand_over(src, dst):
+    dst[...] = src[...]
 
 
 def per_device(n_ctx, n_tp, queries, key_rows, value_rows, selection, out_weight):
@@ -299,7 +360,7 @@
     gk = heads // 2 * HD
     chips = n_ctx // 2
     vmem = pl.BlockSpec(memory_space=pltpu.VMEM)
-    hbm = pl.BlockSpec(memory_space=pl.ANY)
+    hbm = pl.BlockSpec(memory_space=pltpu.HBM)
     dma = pltpu.SemaphoreType.DMA
     held = pl.pallas_call(
         functools.partial(kernel, n_ctx, n_tp, heads),
@@ -310,20 +371,20 @@
             hbm,
         ],
         out_specs=vmem,
-        scratch_shapes=[pltpu.VMEM((n_ctx, 2, BLOCK, HD), jnp.bfloat16) for _ in range(heads)]
-        + [pltpu.VMEM((2, 2, BLOCK, HD), jnp.bfloat16) for _ in range(heads)] + [
+        scratch_shapes=[pltpu.VMEM((n_ctx, BLOCK, HD), jnp.bfloat16) for _ in range(2 * heads)]
+        + [pltpu.VMEM((2, BLOCK, HD), jnp.bfloat16) for _ in range(2 * heads)] + [
             pltpu.VMEM((rows, width), jnp.bfloat16),
             pltpu.VMEM((2, n_tp * gk, cols), jnp.bfloat16),
             pltpu.VMEM((2, rows, n_tp * gk), jnp.bfloat16),
             pltpu.VMEM((rows, cols), jnp.float32),
-            dma((heads, chips)), dma((heads, chips)),
-            dma((heads, chips)), dma((heads, chips)),
+            dma((2 * heads, chips)), dma((2 * heads, chips)),
+            dma((2 * heads, chips)), dma((2 * heads, chips)),
             dma((n_tp,)), dma((n_tp,)), dma((n_tp,)), dma((n_tp,)),
             dma((heads, n_tp)), dma((heads, n_tp)),
             dma((3, heads)),
         ],
         compiler_params=pltpu.CompilerParams(
-            collective_id=0, has_side_effects=True, vmem_limit_bytes=52 * 2**20
+            collective_id=0, has_side_effects=True, vmem_limit_bytes=63 * 2**20
         ),
         cost_estimate=pl.CostEstimate(
             flops=2 * rows * cols * n_tp * width + 12 * rows * BLOCK * width,
@@ -334,9 +395,9 @@
     return pl.pallas_call(
         hand_over,
         out_shape=jax.ShapeDtypeStruct((rows, cols), jnp.bfloat16),
-        in_specs=[hbm],
-        out_specs=hbm,
-        scratch_shapes=[dma((PARTS,))],
+        grid=(PARTS,),
+        in_specs=[pl.BlockSpec((rows // PARTS, cols), lambda n: (n, 0))],
+        out_specs=pl.BlockSpec((rows // PARTS, cols), lambda n: (n, 0)),
     )(held)
 
 

time: 144 us -> 85.2 us (0.59)
  Pallas kernels: 140 us -> 84.9 us
  local copies, waits for them, and re-layouts: 3.8 us -> 0 us
    pallas_call x1, Pallas kernels: 56.8 us -> 5.54 us  [per_device(): pl.pallas_call(hand_over, out_shape=jax.ShapeDtypeStruct((rows, cols), jn...]
    pallas_call x1, Pallas kernels: 83.4 us -> 79.4 us  [per_device(): pl.pallas_call(functools.partial(kernel, n_ctx, n_tp, heads), out_shape=j...]
    unnamed x8 -> x0, local copies, waits for them, and re-layouts: 3.8 us -> none
where the time goes in v3:
time: 85.2 us; the launch traced here: 84.9 us
  Pallas kernels  84.9 us (100%)
    pallas_call x1, Pallas kernels, per_device(): pl.pallas_call(functools.partial(kernel, n_ctx, n_tp, heads), out_shape=j...  79.4 us
    pallas_call x1, Pallas kernels, per_device(): pl.pallas_call(hand_over, out_shape=jax.ShapeDtypeStruct((rows, cols), jn...  5.54 us

profile of v3, /device:TPU:25, one launch (start us, length us, event | category | flops | bytes accessed | tf_op | source)
XLA Modules:
  0.0 84.9 jit_solution(10973823325723644552)
XLA Ops:
  0.0 79.4 %shard_map.55.src = bf16[512,1792]{1,0:T(8,128)(2,1)} custom-call(bf16[512,512]{1,0:T(8,128)(2,1)} %q_hbm.1, bf16[512,512]{1,0:T(8,128)(2,1)} %k_hbm.1, bf16[512,512]{1,0:T(8,128)(2,1)} %v_hbm.1, s32[3,8]{1,0:T(4,128)} %bitcast.1, bf16[512,7168]{1,0:T(8,128)(2,1)} %w_ref.1), custom_call_target="tpu_custom_call" | custom-call | flops 5368709120 | bytes 9437184 | tf_op jit(solution)/shard_map/pallas_call | solution.py:365
  79.4 5.5 %shard_map.56 = bf16[512,1792]{1,0:T(8,128)(2,1)} custom-call(bf16[512,1792]{1,0:T(8,128)(2,1)} %shard_map.55.src), custom_call_target="tpu_custom_call" | custom-call | tf_op jit(solution)/shard_map/pallas_call | solution.py:395

commit v4 on v2

--- a/solution.py
+++ b/solution.py
@@ -10,7 +10,6 @@
 HD = 128
 BLOCK = 512
 NEG = -1e30
-PARTS = 8
 MESH = pl.DeviceIdType.MESH
 SCALE2 = 1.4426950408889634 / HD**0.5
 
@@ -280,18 +279,6 @@
         w_side(p).wait_send()
 
 
-def hand_over(src, dst, sem):
-    step = src.shape[0] // PARTS
-    copies = [
-        pltpu.make_async_copy(src.at[n * step:(n + 1) * step], dst.at[n * step:(n + 1) * step], sem.at[n])
-        for n in range(PARTS)
-    ]
-    for copy in copies:
-        copy.start()
-    for copy in copies:
-        copy.wait()
-
-
 def per_device(n_ctx, n_tp, queries, key_rows, value_rows, selection, out_weight):
     rows, width = queries.shape
     heads = width // HD
@@ -301,7 +288,7 @@
     vmem = pl.BlockSpec(memory_space=pltpu.VMEM)
     hbm = pl.BlockSpec(memory_space=pl.ANY)
     dma = pltpu.SemaphoreType.DMA
-    held = pl.pallas_call(
+    return pl.pallas_call(
         functools.partial(kernel, n_ctx, n_tp, heads),
         out_shape=jax.ShapeDtypeStruct((rows, cols), jnp.bfloat16),
         in_specs=[
@@ -323,7 +310,7 @@
             dma((3, heads)),
         ],
         compiler_params=pltpu.CompilerParams(
-            collective_id=0, has_side_effects=True, vmem_limit_bytes=52 * 2**20
+            collective_id=0, has_side_effects=True, vmem_limit_bytes=63 * 2**20
         ),
         cost_estimate=pl.CostEstimate(
             flops=2 * rows * cols * n_tp * width + 12 * rows * BLOCK * width,
@@ -331,13 +318,6 @@
             transcendentals=3 * rows * BLOCK * heads,
         ),
     )(queries, key_rows, value_rows, selection.T, out_weight)
-    return pl.pallas_call(
-        hand_over,
-        out_shape=jax.ShapeDtypeStruct((rows, cols), jnp.bfloat16),
-        in_specs=[hbm],
-        out_specs=hbm,
-        scratch_shapes=[dma((PARTS,))],
-    )(held)
 
 
 def solution(mesh):

time: 144 us -> 86.3 us (0.60)
  Pallas kernels: 140 us -> 83.3 us
    pallas_call x1 -> x0, Pallas kernels: 56.8 us -> none  [per_device(): pl.pallas_call(hand_over, out_shape=jax.ShapeDtypeStruct((rows, cols), jn...]
    unnamed x8 -> x1, local copies, waits for them, and re-layouts: 3.8 us -> 2.85 us
where the time goes in v4:
time: 86.3 us; the launch traced here: 86.1 us
  Pallas kernels  83.3 us (97%)
  local copies, waits for them, and re-layouts  2.85 us (3%)
    pallas_call x1, Pallas kernels, per_device(): pl.pallas_call(functools.partial(kernel, n_ctx, n_tp, heads), out_shape=j...  83.3 us
    unnamed x1, local copies, waits for them, and re-layouts  2.85 us

profile of v4, /device:TPU:25, one launch (start us, length us, event | category | flops | bytes accessed | tf_op | source)
XLA Modules:
  0.0 86.1 jit_solution(15030092417125562647)
XLA Ops:
  0.0 83.3 %shard_map.55 = bf16[512,1792]{1,0:T(8,128)(2,1)} custom-call(bf16[512,512]{1,0:T(8,128)(2,1)} %q_hbm.1, bf16[512,512]{1,0:T(8,128)(2,1)} %k_hbm.1, bf16[512,512]{1,0:T(8,128)(2,1)} %v_hbm.1, s32[3,8]{1,0:T(4,128)} %bitcast.1, bf16[512,7168]{1,0:T(8,128)(2,1)} %w_ref.1), custom_call_target="tpu_custom_call" | custom-call | flops 5368709120 | bytes 9437184 | tf_op jit(solution)/shard_map/pallas_call | solution.py:291
  83.3 2.8 %copy.7 = bf16[512,1792]{1,0:T(8,128)(2,1)} copy(bf16[512,1792]{1,0:T(8,128)(2,1)} %shard_map.55) | data formatting | bytes 3670016
